TPU v7x, 32 devices: a whole 2x2x4 slice. The times are simulated.
32 devices in a mesh: branch: 4 (over y, x), row: 8 (over z, core).
Axes of the slice: x: 2, y: 2, z: 4, core: 2. Of those that a mesh axis runs over, the one named last changes fastest.
Arguments:
- root_cov: bfloat16 [2304, 2304], P('row', 'branch')
- diag_factor: float32 [4, 3, 576, 576], P('branch')
- panel_factor: float32 [4, 3, 2304, 576], P('branch', None, 'row'), may hold values from -0.009765625 to 0.009765625
- chain_factor: float32 [4, 2, 576, 576], P('branch'), may hold values from -0.25 to 0.25
- panel_tiles: int32 [4, 3], P('branch'), may hold values from 0 to 3, as said below
Outputs:
- panel_cov: float32 [4, 3, 2304, 576], P('branch', None, 'row')
- block_cov: float32 [4, 5, 576, 576], P('branch')
Inputs may be any that keep to these rules, and one draw needn't show every extreme that they name: `panel_tiles`: the entries of a row are distinct; the first 2 and the first 1 entries of a row are the level-two and level-three patterns.
All inputs are finite; a program needn't handle non-finite values.
Results may differ from a plain program's by a relative error of at most 0.0029.
Values may be sent and summed in bfloat16 or wider, within the bound.
A program may use at most 192 MiB of HBM per device.

v0:
```python
import jax
import jax.numpy as jnp
from jax import lax
from jax.sharding import PartitionSpec as P

HIGHEST = lax.Precision.HIGHEST


def product(left_mat, right_mat):
    return jnp.dot(left_mat, right_mat, precision=HIGHEST, preferred_element_type=jnp.float32)


def on_device(root_cov, diag_factor, panel_factor, chain_factor, panel_tiles):
    node_width = diag_factor.shape[-1]
    rows_here = panel_factor.shape[2]
    per_tile = node_width // rows_here
    tile_total = lax.axis_size("row") // per_tile
    counts = (3 * tile_total // 4, tile_total // 2, tile_total // 4)
    root_rows = lax.all_gather(root_cov, "branch", axis=1, tiled=True)
    my_tile = lax.axis_index("row") // per_tile
    identity = jnp.eye(node_width, dtype=jnp.float32)
    panels = []
    blocks = []
    crosses = []
    for layer_index in range(3):
        inverse = jax.scipy.linalg.solve_triangular(
            diag_factor[0, layer_index], identity, lower=True
        )
        gram = product(inverse.T, inverse)
        chosen = jnp.any(panel_tiles[0, : counts[layer_index]] == my_tile)
        scaled = jnp.where(chosen, product(panel_factor[0, layer_index], inverse), 0.0)
        gathered = jnp.dot(
            root_rows,
            lax.all_gather(scaled.astype(jnp.bfloat16), "row", axis=0, tiled=True),
            preferred_element_type=jnp.float32,
        )
        if layer_index == 0:
            panel = -jnp.where(chosen, gathered, 0.0)
            block = gram - lax.psum(product(scaled.T, panel), "row")
        else:
            previous_panel = panels[-1]
            previous_block = blocks[-1]
            scaled_chain = product(chain_factor[0, layer_index - 1], inverse)
            panel = -jnp.where(chosen, gathered + product(previous_panel, scaled_chain), 0.0)
            cross_sum, block_sum = lax.psum(
                (product(previous_panel.T, scaled), product(scaled.T, panel)), "row"
            )
            cross = -(cross_sum + product(previous_block, scaled_chain))
            block = gram - block_sum - product(scaled_chain.T, cross)
            crosses.append(cross)
        panels.append(panel)
        blocks.append(block)
    return (jnp.stack(panels)[None], jnp.stack(blocks + crosses)[None])


def solution(mesh):
    in_specs = (
        P("row", "branch"),
        P("branch", None, None, None),
        P("branch", None, "row", None),
        P("branch", None, None, None),
        P("branch", None),
    )
    out_specs = (P("branch", None, "row", None), P("branch", None, None, None))
    return jax.shard_map(
        on_device, mesh=mesh, in_specs=in_specs, out_specs=out_specs, check_vma=False
    )
```

profile of v0, /device:TPU:0, one launch (start us, length us, event | category | flops | bytes accessed | tf_op | source)
XLA Modules:
  0.0 502.8 jit_solution(1767455906042671020)
XLA Ops:
  8.1 4.2 bitcast_select_fusion.2
  13.5 11.7 %while.6 = (s32[]{:T(128)}, f32[576,576]{1,0:T(8,128)}, s32[4,2]{0,1:T(2,128)S(1)}, f32[4,128,128]{2,1,0:T(8,128)S(1)}, s32[]{:T(128)}) while((s32[]{:T(128)}, f32[576,576]{1,0:T(8,128)}, s32[4,2]{0,1:T(2,128)S(1)}, f32[4,128,128]{2,1,0:T(8,128)S(1)}, s32[]{:T(128)}) %tuple.93), condition=%wide.while_cond, body=%wide.while_body.sunk | while | flops 2 | bytes 131189 | solution.py:26
  14.2 2.2 bitcast_dynamic-update-slice_fusion.11
  17.1 2.3 bitcast_dynamic-update-slice_fusion.11
  20.0 2.2 bitcast_dynamic-update-slice_fusion.11
  22.9 2.2 bitcast_dynamic-update-slice_fusion.11
  25.2 1.4 triangular_solve.404
  26.6 11.7 %while.7 = (s32[]{:T(128)}, f32[576,576]{1,0:T(8,128)}, s32[4,2]{0,1:T(2,128)S(1)}, f32[4,128,128]{2,1,0:T(8,128)S(1)}, s32[]{:T(128)}) while((s32[]{:T(128)}, f32[576,576]{1,0:T(8,128)}, s32[4,2]{0,1:T(2,128)S(1)}, f32[4,128,128]{2,1,0:T(8,128)S(1)}, s32[]{:T(128)}) %tuple.94), condition=%wide.while_cond.clone, body=%wide.while_body.clone.sunk | while | flops 2 | bytes 131189 | solution.py:26
  27.2 2.2 bitcast_dynamic-update-slice_fusion.12
  30.2 2.2 bitcast_dynamic-update-slice_fusion.12
  33.1 2.2 bitcast_dynamic-update-slice_fusion.12
  36.0 2.2 bitcast_dynamic-update-slice_fusion.12
  38.2 1.5 fusion.104
  39.7 0.9 pad_maximum_fusion
  40.6 50.6 %custom-call.5 = f32[5,128,128]{1,2,0:T(8,128)} custom-call(f32[5,128,128]{2,1,0:T(8,128)} %get-tuple-element.95), custom_call_target="InvertDiagBlocksLowerTriangular" | custom-call | tf_op jit(solution)/shard_map/jit(_solve_triangular)/triangular_solve | solution.py:26
  91.2 1.2 constant_dynamic-update-slice_fusion.3
  92.4 1.2 convolution_subtract_fusion.6
  94.4 1.2 constant_dynamic-update-slice_fusion.2
  95.7 1.5 convolution_subtract_fusion.5
  97.6 1.9 convolution_subtract_fusion.9
  99.9 2.0 fusion.42
  102.2 4.1 convolution_select_fusion.2
  108.3 49.9 %custom-call.6 = f32[5,128,128]{1,2,0:T(8,128)S(1)} custom-call(f32[5,128,128]{2,1,0:T(8,128)} %get-tuple-element.96), custom_call_target="InvertDiagBlocksLowerTriangular" | custom-call | tf_op jit(solution)/shard_map/jit(_solve_triangular)/triangular_solve | solution.py:26
  159.3 1.3 convolution_subtract_fusion.4
  161.0 1.5 convolution_subtract_fusion.3
  162.9 1.9 convolution_subtract_fusion.8
  165.2 2.0 fusion.39
  167.6 4.1 convolution_select_fusion.1
  173.0 11.8 %while.8 = (s32[]{:T(128)}, f32[576,576]{1,0:T(8,128)}, s32[4,2]{0,1:T(2,128)S(1)}, f32[4,128,128]{2,1,0:T(8,128)S(1)}, s32[]{:T(128)}) while((s32[]{:T(128)}, f32[576,576]{1,0:T(8,128)}, s32[4,2]{0,1:T(2,128)S(1)}, f32[4,128,128]{2,1,0:T(8,128)S(1)}, s32[]{:T(128)}) %tuple.95), condition=%wide.while_cond.clone.1, body=%wide.while_body.clone.1.sunk | while | flops 2 | bytes 131189 | solution.py:26
  173.6 2.3 bitcast_dynamic-update-slice_fusion.13
  176.6 2.3 bitcast_dynamic-update-slice_fusion.13
  179.5 2.3 bitcast_dynamic-update-slice_fusion.13
  182.5 2.3 bitcast_dynamic-update-slice_fusion.13
  184.8 49.1 %custom-call.7 = f32[5,128,128]{1,2,0:T(8,128)S(1)} custom-call(f32[5,128,128]{2,1,0:T(8,128)S(1)} %pad_maximum_fusion.2), custom_call_target="InvertDiagBlocksLowerTriangular" | custom-call | tf_op jit(solution)/shard_map/jit(_solve_triangular)/triangular_solve | solution.py:26
  234.0 1.5 constant_dynamic-update-slice_fusion.11
  235.5 1.4 convolution_subtract_fusion.2
  237.3 1.5 convolution_subtract_fusion.1
  239.3 1.9 convolution_subtract_fusion.7
  241.5 2.0 fusion.36
  243.9 3.4 convolution_select_fusion
  249.2 6.8 %fusion.2 = f32[576,576]{1,0:T(8,128)} fusion(f32[576,576]{0,1:T(8,128)S(1)} %convolution_dynamic-update-slice_fusion.1, f32[1,2,576,576]{3,2,1,0:T(8,128)} %param.10), kind=kOutput, calls=%fused_computation.15 | convolution fusion | flops 2293235712 | bytes 4128768 | tf_op jit(solution)/shard_map/dot_general | solution.py:10
  256.0 5.3 %fusion = f32[576,576]{1,0:T(8,128)} fusion(f32[576,576]{0,1:T(8,128)S(1)} %convolution_dynamic-update-slice_fusion, f32[1,2,576,576]{3,2,1,0:T(8,128)S(1)} %copy-done.26), kind=kOutput, calls=%fused_computation.12 | convolution fusion | flops 2293235712 | bytes 4276224 | tf_op jit(solution)/shard_map/dot_general | solution.py:10
  261.3 3.2 copy.16
  264.6 4.0 reshape.47
  268.7 4.2 fusion.11
  273.8 3.9 fusion.117
  277.7 3.6 convolution_bitcast_fusion.1
  281.3 3.0 fusion.10
  284.4 3.9 fusion.123
  288.3 4.3 fusion.119
  292.6 3.9 fusion.120
  296.5 3.6 convolution_bitcast_fusion
  300.1 2.3 fusion.8
  303.3 3.9 fusion.122
  307.2 5.5 %fusion.118 = f32[576,576]{1,0:T(8,128)} fusion(f32[576,576]{0,1:T(8,128)S(1)} %convolution_dynamic-update-slice_fusion.1), kind=kOutput, calls=%fused_computation.195 | convolution fusion | flops 2293235712 | bytes 2654208 | tf_op jit(solution)/shard_map/dot_general | solution.py:10
  312.6 5.3 %fusion.121 = f32[576,576]{1,0:T(8,128)} fusion(f32[576,576]{0,1:T(8,128)S(1)} %convolution_dynamic-update-slice_fusion), kind=kOutput, calls=%fused_computation.198 | convolution fusion | flops 2293235712 | bytes 2654208 | tf_op jit(solution)/shard_map/dot_general | solution.py:10
  318.0 1.5 maximum_bitcast_fusion
  319.5 148.9 %all-reduce.5.cloned.1.call-done = (f32[576,576]{1,0:T(8,128)}, f32[576,576]{1,0:T(8,128)}, f32[576,576]{1,0:T(8,128)}, f32[576,576]{1,0:T(8,128)}, f32[576,576]{1,0:T(8,128)}) async-done(((f32[576,576]{1,0:T(8,128)}, f32[576,576]{1,0:T(8,128)}, f32[576,576]{1,0:T(8,128)}, f32[576,576]{1,0:T(8,128)}, f32[576,576]{1,0:T(8,128)}), (f32[576,576]{1,0:T(8,128)}, f32[576,576]{1,0:T(8,128)}, f32[576,576]{1,0:T(8,128)}, ...) | async-done | bytes 6635536 | tf_op jit(solution)/shard_map/psum | solution.py:39
  468.3 6.7 %bitcast_dynamic-update-slice_fusion.7 = (f32[5,576,576]{2,1,0:T(8,128)S(1)}, f32[576,576]{1,0:T(8,128)S(1)}) fusion(f32[576,576]{1,0:T(8,128)} %get-tuple-element.50, f32[576,576]{0,1:T(8,128)} %copy-done.9), kind=kOutput, calls=%fused_computation.11 | convolution fusion | flops 2293567488 | bytes 7372800 | tf_op jit(solution)/shard_map/dot_general | solution.py:10
  475.0 4.4 add_negate_fusion.1
  479.5 4.2 bitcast_dynamic-update-slice_fusion.6
  483.8 4.3 add_negate_fusion
  488.1 4.5 bitcast_dynamic-update-slice_fusion.5
  492.8 3.0 copy-done.31
  (137 shorter events, 23.1 us)
Async XLA Ops:
  7.2 254.2 %all-gather.12.cloned.1.call-start = ((), (), s32[]{:S(2)}) async-start(), calls=%async_computation.3 | async-start | bytes 1843200 | tf_op jit(solution)/shard_map/all_gather | solution.py:19
  7.9 260.7 %all-gather.6.cloned.1.call-start = ((), (), s32[]{:S(2)}) async-start(), calls=%async_computation | async-start | bytes 3317760 | tf_op jit(solution)/shard_map/all_gather | solution.py:34
  8.1 157.1 %copy-start.7 = (f32[576,576]{0,1:T(8,128)}, f32[576,576]{0,1:T(8,128)S(1)}, u32[]{:S(2)}) copy-start(f32[576,576]{0,1:T(8,128)S(1)} %fusion.6) | copy-start | bytes 3981316
  12.3 1.2 copy-start.25
  12.3 28.3 %copy-start.24 = (f32[576,576]{1,0:T(8,128)}, f32[576,576]{1,0:T(8,128)S(1)}, u32[]{:S(2)}) copy-start(f32[576,576]{1,0:T(8,128)S(1)} %get-tuple-element.185) | copy-start | bytes 3981316
  39.7 54.0 %copy-start.34 = (s32[1,3]{1,0:T(1,128)S(1)}, s32[1,3]{1,0:T(1,128)}, u32[]{:S(2)}) copy-start(s32[1,3]{1,0:T(1,128)} %param.11) | copy-start | bytes 40
  93.7 3.5 copy-start.32
  102.2 4.1 copy-start.9
  106.4 0.9 copy-start.18
  108.0 169.6 %all-gather.8.cloned.1.call-start = ((), (), s32[]{:S(2)}) async-start(), calls=%async_computation.1 | async-start | bytes 3317760 | tf_op jit(solution)/shard_map/all_gather | solution.py:34
  171.6 13.2 %copy-start.10 = (f32[576,288]{0,1:T(8,128)}, f32[576,288]{0,1:T(8,128)S(1)}, u32[]{:S(2)}) copy-start(f32[576,288]{0,1:T(8,128)S(1)} %convolution_select_fusion.1) | copy-start | bytes 1990660
  171.6 13.2 %copy-start.33 = (f32[1,128,128]{2,1,0:T(8,128)S(1)}, f32[1,128,128]{2,1,0:T(8,128)}, u32[]{:S(2)}) copy-start(f32[1,128,128]{2,1,0:T(8,128)} %get-tuple-element.66) | copy-start | bytes 196612
  172.5 124.0 %all-gather.10.cloned.1.call-start = ((), (), s32[]{:S(2)}) async-start(), calls=%async_computation.2 | async-start | bytes 3317760 | tf_op jit(solution)/shard_map/all_gather | solution.py:34
  234.0 3.3 copy-start.8
  247.3 0.9 copy-start.12
  249.0 219.3 %all-reduce.5.cloned.1.call-start = ((), (), s32[]{:S(2)}) async-start(), calls=%async_computation.4 | async-start | bytes 14745600 | tf_op jit(solution)/shard_map/psum | solution.py:39
  249.2 6.8 %copy-start.26 = (f32[1,2,576,576]{3,2,1,0:T(8,128)S(1)}, f32[1,2,576,576]{3,2,1,0:T(8,128)}, u32[]{:S(2)}) copy-start(f32[1,2,576,576]{3,2,1,0:T(8,128)} %param.10) | copy-start | bytes 7962628
  268.6 5.1 %copy-start.19 = (f32[576,288]{0,1:T(8,128)S(1)}, f32[576,288]{0,1:T(8,128)}, u32[]{:S(2)}) copy-start(f32[576,288]{0,1:T(8,128)} %copy-done.18) | copy-start | bytes 1990660
  272.9 0.9 copy-start.15
  277.7 3.7 copy-start.2
  277.7 3.7 copy-start.16
  281.3 3.0 copy-start.13
  284.4 8.2 %copy-start.4 = (f32[288,576]{1,0:T(8,128)}, f32[288,576]{1,0:T(8,128)S(1)}, u32[]{:S(2)}) copy-start(f32[288,576]{1,0:T(8,128)S(1)} %fusion.10) | copy-start | bytes 1990660
  284.4 3.9 copy-start.11
  296.5 3.6 copy-start
  296.5 3.6 copy-start.5
  300.1 3.2 copy-start.14
  302.4 0.9 copy-start.20
  312.6 5.3 %copy-start.6 = (f32[288,576]{1,0:T(8,128)S(1)}, f32[288,576]{1,0:T(8,128)}, u32[]{:S(2)}) copy-start(f32[288,576]{1,0:T(8,128)} %copy-done.4) | copy-start | bytes 1990660
  312.6 5.3 %copy-start.17 = (f32[576,288]{0,1:T(8,128)S(1)}, f32[576,288]{0,1:T(8,128)}, u32[]{:S(2)}) copy-start(f32[576,288]{0,1:T(8,128)} %copy-done.15) | copy-start | bytes 1990660
  312.6 5.3 %copy-start.21 = (f32[288,576]{1,0:T(8,128)S(1)}, f32[288,576]{1,0:T(8,128)}, u32[]{:S(2)}) copy-start(f32[288,576]{1,0:T(8,128)} %copy-done.20) | copy-start | bytes 1990660
  468.3 6.7 %copy-start.3 = (f32[576,576]{1,0:T(8,128)S(1)}, f32[576,576]{1,0:T(8,128)}, u32[]{:S(2)}) copy-start(f32[576,576]{1,0:T(8,128)} %fusion.2) | copy-start | bytes 3981316
  468.3 6.7 %copy-start.30 = (f32[576,576]{1,0:T(8,128)S(1)}, f32[576,576]{1,0:T(8,128)}, u32[]{:S(2)}) copy-start(f32[576,576]{1,0:T(8,128)} %get-tuple-element.52) | copy-start | bytes 3981316
  475.0 4.5 copy-start.23
  475.0 4.5 copy-start.29
  479.5 4.2 copy-start.1
  479.5 4.2 copy-start.28
  483.8 4.3 copy-start.22
  483.8 4.3 copy-start.27
  492.8 3.1 copy-start.31
Sparse Core Ops, SparseCore 0:
  9.8 32.9 all-gather.11
  108.2 39.4 all-gather.5
  172.6 39.3 all-gather.7
  249.1 39.3 all-gather.9
  307.3 160.9 all-reduce.4
where the time goes:
time: 512 us; the launch traced here: 503 us
  other arithmetic  162 us (32%)
  waiting for transfers between devices  150 us (29%)
  matrix products  124 us (24%)
  local copies, waits for them, and re-layouts  51.7 us (10%)
  between operations  15.1 us (3%)
    another operation x10, other arithmetic, on_device(): jax.scipy.linalg.solve_triangular(diag_factor[0, layer_index], identity,...  156 us
    psum x1, waiting for transfers between devices, on_device(): block = gram - lax.psum(product(scaled.T, panel), 'row')  149 us
    dot_general x19, matrix products, product(): jnp.dot(left_mat, right_mat, precision=HIGHEST, preferred_element_type=jn...  83.7 us
    another operation x43, local copies, waits for them, and re-layouts, on_device(): jax.scipy.linalg.solve_triangular(diag_factor[0, layer_index], identity,...  37 us
    another operation x27, matrix products, on_device(): jax.scipy.linalg.solve_triangular(diag_factor[0, layer_index], identity,...  28.5 us
    dot_general x3, matrix products, on_device(): jnp.dot(root_rows, lax.all_gather(scaled.astype(jnp.bfloat16), 'row', axi...  11.5 us
    unnamed x72, local copies, waits for them, and re-layouts  11.3 us
  transfers between devices with their start and end apart: 5, of which 1 were waited for; matrix products, arithmetic and copies ran while one was open for 59% of the time, Pallas kernels for 0%

commit v1 on v0

--- a/solution.py
+++ b/solution.py
@@ -36,7 +36,7 @@
         )
         if layer_index == 0:
             panel = -jnp.where(chosen, gathered, 0.0)
-            block = gram - lax.psum(product(scaled.T, panel), "row")
+            block = gram - jnp.sum(lax.all_gather(product(scaled.T, panel), "row"), axis=0)
         else:
             previous_panel = panels[-1]
             previous_block = blocks[-1]

time: 512 us -> 570 us (1.11)
  waiting for transfers between devices: 150 us -> 197 us
  other arithmetic: 162 us -> 168 us
    all_gather x0 -> x1, waiting for transfers between devices: none -> 79.6 us  [on_device(): lax.all_gather(product(scaled.T, panel), 'row')]
    psum x1, waiting for transfers between devices: 149 us -> 117 us  [on_device(): lax.psum((product(previous_panel.T, scaled), product(scaled.T, panel)), '...]
    reduce_sum x0 -> x1, other arithmetic: none -> 6.54 us  [on_device(): jnp.sum(lax.all_gather(product(scaled.T, panel), 'row'), axis=0)]
  transfers between devices with their start and end apart: 5 -> 6, of which waited for: 1 -> 2; matrix products, arithmetic and copies ran while one was open for 59% -> 57% of each run, Pallas kernels for 0% -> 0%
where the time goes in v1:
time: 570 us; the launch traced here: 561 us
  waiting for transfers between devices  197 us (35%)
  other arithmetic  168 us (29%)
  matrix products  128 us (22%)
  local copies, waits for them, and re-layouts  51.1 us (9%)
  between operations  15.1 us (3%)
    another operation x10, other arithmetic, on_device(): jax.scipy.linalg.solve_triangular(diag_factor[0, layer_index], identity,...  156 us
    psum x1, waiting for transfers between devices, on_device(): lax.psum((product(previous_panel.T, scaled), product(scaled.T, panel)), '...  117 us
    dot_general x19, matrix products, product(): jnp.dot(left_mat, right_mat, precision=HIGHEST, preferred_element_type=jn...  87.9 us
    all_gather x1, waiting for transfers between devices, on_device(): lax.all_gather(product(scaled.T, panel), 'row')  79.6 us
    another operation x43, local copies, waits for them, and re-layouts, on_device(): jax.scipy.linalg.solve_triangular(diag_factor[0, layer_index], identity,...  37.5 us
    another operation x27, matrix products, on_device(): jax.scipy.linalg.solve_triangular(diag_factor[0, layer_index], identity,...  28.6 us
    dot_general x3, matrix products, on_device(): jnp.dot(root_rows, lax.all_gather(scaled.astype(jnp.bfloat16), 'row', axi...  12 us
  transfers between devices with their start and end apart: 6, of which 2 were waited for; matrix products, arithmetic and copies ran while one was open for 57% of the time, Pallas kernels for 0%

profile of v1, /device:TPU:0, one launch (start us, length us, event | category | flops | bytes accessed | tf_op | source)
XLA Modules:
  0.0 561.4 jit_solution(2982065199573679443)
XLA Ops:
  8.1 4.2 bitcast_select_fusion.2
  13.4 12.0 %while.6 = (s32[]{:T(128)}, f32[576,576]{1,0:T(8,128)}, s32[4,2]{0,1:T(2,128)S(1)}, f32[4,128,128]{2,1,0:T(8,128)S(1)}, s32[]{:T(128)}) while((s32[]{:T(128)}, f32[576,576]{1,0:T(8,128)}, s32[4,2]{0,1:T(2,128)S(1)}, f32[4,128,128]{2,1,0:T(8,128)S(1)}, s32[]{:T(128)}) %tuple.95), condition=%wide.while_cond, body=%wide.while_body.sunk | while | flops 2 | bytes 131189 | solution.py:26
  14.1 2.3 bitcast_dynamic-update-slice_fusion.11
  17.1 2.3 bitcast_dynamic-update-slice_fusion.11
  20.2 2.3 bitcast_dynamic-update-slice_fusion.11
  23.2 2.3 bitcast_dynamic-update-slice_fusion.11
  25.5 1.4 triangular_solve.404
  26.9 11.5 %while.7 = (s32[]{:T(128)}, f32[576,576]{1,0:T(8,128)}, s32[4,2]{0,1:T(2,128)S(1)}, f32[4,128,128]{2,1,0:T(8,128)S(1)}, s32[]{:T(128)}) while((s32[]{:T(128)}, f32[576,576]{1,0:T(8,128)}, s32[4,2]{0,1:T(2,128)S(1)}, f32[4,128,128]{2,1,0:T(8,128)S(1)}, s32[]{:T(128)}) %tuple.96), condition=%wide.while_cond.clone, body=%wide.while_body.clone.sunk | while | flops 2 | bytes 131189 | solution.py:26
  27.6 2.2 bitcast_dynamic-update-slice_fusion.12
  30.4 2.2 bitcast_dynamic-update-slice_fusion.12
  33.4 2.2 bitcast_dynamic-update-slice_fusion.12
  36.2 2.2 bitcast_dynamic-update-slice_fusion.12
  38.5 1.5 fusion.104
  40.8 50.6 %custom-call.5 = f32[5,128,128]{1,2,0:T(8,128)} custom-call(f32[5,128,128]{2,1,0:T(8,128)} %get-tuple-element.94), custom_call_target="InvertDiagBlocksLowerTriangular" | custom-call | tf_op jit(solution)/shard_map/jit(_solve_triangular)/triangular_solve | solution.py:26
  91.4 1.2 constant_dynamic-update-slice_fusion.3
  92.7 1.2 convolution_subtract_fusion.6
  94.6 1.2 constant_dynamic-update-slice_fusion.2
  95.8 1.5 convolution_subtract_fusion.5
  97.8 1.9 convolution_subtract_fusion.9
  100.0 2.0 fusion.42
  102.4 4.1 convolution_select_fusion.2
  108.4 49.9 %custom-call.6 = f32[5,128,128]{1,2,0:T(8,128)S(1)} custom-call(f32[5,128,128]{2,1,0:T(8,128)} %get-tuple-element.95), custom_call_target="InvertDiagBlocksLowerTriangular" | custom-call | tf_op jit(solution)/shard_map/jit(_solve_triangular)/triangular_solve | solution.py:26
  159.4 1.3 convolution_subtract_fusion.4
  161.1 1.5 convolution_subtract_fusion.3
  163.0 1.9 convolution_subtract_fusion.8
  165.3 2.0 fusion.39
  167.7 4.0 convolution_select_fusion.1
  173.0 12.1 %while.8 = (s32[]{:T(128)}, f32[576,576]{1,0:T(8,128)}, s32[4,2]{0,1:T(2,128)S(1)}, f32[4,128,128]{2,1,0:T(8,128)S(1)}, s32[]{:T(128)}) while((s32[]{:T(128)}, f32[576,576]{1,0:T(8,128)}, s32[4,2]{0,1:T(2,128)S(1)}, f32[4,128,128]{2,1,0:T(8,128)S(1)}, s32[]{:T(128)}) %tuple.97), condition=%wide.while_cond.clone.1, body=%wide.while_body.clone.1.sunk | while | flops 2 | bytes 131189 | solution.py:26
  173.7 2.3 bitcast_dynamic-update-slice_fusion.13
  176.7 2.3 bitcast_dynamic-update-slice_fusion.13
  179.8 2.3 bitcast_dynamic-update-slice_fusion.13
  182.8 2.3 bitcast_dynamic-update-slice_fusion.13
  185.2 49.1 %custom-call.7 = f32[5,128,128]{1,2,0:T(8,128)S(1)} custom-call(f32[5,128,128]{2,1,0:T(8,128)S(1)} %pad_maximum_fusion.2), custom_call_target="InvertDiagBlocksLowerTriangular" | custom-call | tf_op jit(solution)/shard_map/jit(_solve_triangular)/triangular_solve | solution.py:26
  234.4 1.5 constant_dynamic-update-slice_fusion.11
  235.9 1.4 convolution_subtract_fusion.2
  237.7 1.5 convolution_subtract_fusion.1
  239.6 1.9 convolution_subtract_fusion.7
  241.9 2.0 fusion.36
  244.2 3.4 convolution_select_fusion
  249.5 3.2 copy.16
  252.7 3.9 reshape.48
  256.6 4.3 fusion.11
  261.7 3.9 fusion.117
  265.9 6.9 %fusion.2 = f32[576,576]{1,0:T(8,128)} fusion(f32[576,576]{0,1:T(8,128)S(1)} %convolution_dynamic-update-slice_fusion.1, f32[1,2,576,576]{3,2,1,0:T(8,128)} %param.10), kind=kOutput, calls=%fused_computation.15 | convolution fusion | flops 2293235712 | bytes 4128768 | tf_op jit(solution)/shard_map/dot_general | solution.py:10
  272.7 5.3 fusion
  278.0 3.6 convolution_bitcast_fusion.1
  281.7 3.2 fusion.10
  284.9 3.9 fusion.123
  288.8 3.9 fusion.119
  292.7 3.9 fusion.120
  296.6 4.1 convolution_bitcast_fusion
  300.7 2.3 fusion.8
  304.0 4.4 fusion.122
  308.4 5.3 fusion.118
  313.7 5.3 fusion.121
  319.0 1.5 maximum_bitcast_fusion
  320.5 79.6 %all-gather.14.cloned.1.call-done = f32[4608,576]{1,0:T(8,128)} async-done(((f32[576,576]{1,0:T(8,128)}), f32[4608,576]{1,0:T(8,128)}) %all-gather.14.cloned.1.call-update) | async-done | bytes 10616848 | tf_op jit(solution)/shard_map/all_gather | solution.py:39
  400.1 6.5 %reduce_sum.9 = f32[576,576]{1,0:T(8,128)} reduce(f32[8,576,576]{2,1,0:T(8,128)} %bitcast.219, f32[]{:T(128)} %constant.35.clone.1), dimensions={0}, to_apply=%region_2.4 | reduce | flops 2322432 | bytes 11943940 | tf_op jit(solution)/shard_map/reduce_sum | solution.py:39
  406.6 7.0 %bitcast_dynamic-update-slice_fusion.7 = (f32[5,576,576]{2,1,0:T(8,128)}, f32[576,576]{1,0:T(8,128)}) fusion(f32[576,576]{1,0:T(8,128)} %reduce_sum.9, f32[576,576]{0,1:T(8,128)S(1)} %copy-done.10), kind=kOutput, calls=%fused_computation.11 | convolution fusion | flops 2293567488 | bytes 7225344 | tf_op jit(solution)/shard_map/dot_general | solution.py:10
  413.6 117.0 %all-reduce.5.cloned.1.call-done = (f32[576,576]{1,0:T(8,128)}, f32[576,576]{1,0:T(8,128)}, f32[576,576]{1,0:T(8,128)}, f32[576,576]{1,0:T(8,128)}) async-done(((f32[576,576]{1,0:T(8,128)}, f32[576,576]{1,0:T(8,128)}, f32[576,576]{1,0:T(8,128)}, f32[576,576]{1,0:T(8,128)}), (f32[576,576]{1,0:T(8,128)}, f32[576,576]{1,0:T(8,128)}, f32[576,576]{1,0:T(8,128)}, ...) | async-done | bytes 5308432 | tf_op jit(solution)/shard_map/psum | solution.py:45
  530.6 6.1 %add_negate_fusion.1 = f32[576,576]{1,0:T(8,128)S(1)} fusion(f32[576,576]{1,0:T(8,128)} %get-tuple-element.51, f32[576,576]{1,0:T(8,128)} %get-tuple-element.91, f32[576,576]{1,0:T(8,128)S(1)} %copy-done.3), kind=kOutput, calls=%fused_computation.21 | convolution fusion | flops 2293899264 | bytes 5308416 | tf_op jit(solution)/shard_map/dot_general | solution.py:10
  536.8 5.3 bitcast_dynamic-update-slice_fusion.6
  542.1 4.4 add_negate_fusion
  546.6 5.4 bitcast_dynamic-update-slice_fusion.5
  (139 shorter events, 26.4 us)
Async XLA Ops:
  7.2 242.3 %all-gather.16.cloned.1.call-start = ((), (), s32[]{:S(2)}) async-start(), calls=%async_computation.4 | async-start | bytes 1843200 | tf_op jit(solution)/shard_map/all_gather | solution.py:19
  7.9 248.7 %all-gather.8.cloned.1.call-start = ((), (), s32[]{:S(2)}) async-start(), calls=%async_computation | async-start | bytes 3317760 | tf_op jit(solution)/shard_map/all_gather | solution.py:34
  8.1 157.2 %copy-start.7 = (f32[576,576]{0,1:T(8,128)}, f32[576,576]{0,1:T(8,128)S(1)}, u32[]{:S(2)}) copy-start(f32[576,576]{0,1:T(8,128)S(1)} %fusion.6) | copy-start | bytes 3981316
  12.3 1.2 copy-start.26
  12.3 28.6 %copy-start.25 = (f32[576,576]{1,0:T(8,128)}, f32[576,576]{1,0:T(8,128)S(1)}, u32[]{:S(2)}) copy-start(f32[576,576]{1,0:T(8,128)S(1)} %get-tuple-element.184) | copy-start | bytes 3981316
  39.9 54.0 %copy-start.33 = (s32[1,3]{1,0:T(1,128)S(1)}, s32[1,3]{1,0:T(1,128)}, u32[]{:S(2)}) copy-start(s32[1,3]{1,0:T(1,128)} %param.11) | copy-start | bytes 40
  93.9 3.5 copy-start.31
  102.4 4.1 copy-start.9
  106.5 0.9 copy-start.19
  108.2 169.8 %all-gather.10.cloned.1.call-start = ((), (), s32[]{:S(2)}) async-start(), calls=%async_computation.1 | async-start | bytes 3317760 | tf_op jit(solution)/shard_map/all_gather | solution.py:34
  171.7 13.5 %copy-start.11 = (f32[576,288]{0,1:T(8,128)}, f32[576,288]{0,1:T(8,128)S(1)}, u32[]{:S(2)}) copy-start(f32[576,288]{0,1:T(8,128)S(1)} %convolution_select_fusion.1) | copy-start | bytes 1990660
  171.7 13.4 %copy-start.32 = (f32[1,128,128]{2,1,0:T(8,128)S(1)}, f32[1,128,128]{2,1,0:T(8,128)}, u32[]{:S(2)}) copy-start(f32[1,128,128]{2,1,0:T(8,128)} %get-tuple-element.65) | copy-start | bytes 196612
  172.6 124.0 %all-gather.12.cloned.1.call-start = ((), (), s32[]{:S(2)}) async-start(), calls=%async_computation.2 | async-start | bytes 3317760 | tf_op jit(solution)/shard_map/all_gather | solution.py:34
  234.3 3.3 copy-start.8
  247.7 0.9 copy-start.13
  249.4 150.7 %all-gather.14.cloned.1.call-start = ((), (), s32[]{:S(2)}) async-start(), calls=%async_computation.3 | async-start | bytes 13271040 | tf_op jit(solution)/shard_map/all_gather | solution.py:39
  256.6 5.2 copy-start.20
  260.9 0.9 copy-start.16
  265.6 265.0 %all-reduce.5.cloned.1.call-start = ((), (), s32[]{:S(2)}) async-start(), calls=%async_computation.5 | async-start | bytes 11796480 | tf_op jit(solution)/shard_map/psum | solution.py:45
  265.8 6.9 %copy-start.27 = (f32[1,2,576,576]{3,2,1,0:T(8,128)S(1)}, f32[1,2,576,576]{3,2,1,0:T(8,128)}, u32[]{:S(2)}) copy-start(f32[1,2,576,576]{3,2,1,0:T(8,128)} %param.10) | copy-start | bytes 7962628
  278.0 3.6 copy-start.2
  278.0 3.7 copy-start.17
  281.7 3.2 copy-start.14
  284.9 7.8 %copy-start.4 = (f32[288,576]{1,0:T(8,128)}, f32[288,576]{1,0:T(8,128)S(1)}, u32[]{:S(2)}) copy-start(f32[288,576]{1,0:T(8,128)S(1)} %fusion.10) | copy-start | bytes 1990660
  284.9 3.9 copy-start.12
  296.6 4.1 copy-start
  296.6 4.1 copy-start.5
  300.7 3.2 copy-start.15
  303.0 0.9 copy-start.21
  313.7 5.3 copy-start.6
  313.7 5.3 copy-start.18
  313.7 5.3 copy-start.22
  400.1 6.5 %copy-start.10 = (f32[576,576]{0,1:T(8,128)S(1)}, f32[576,576]{0,1:T(8,128)}, u32[]{:S(2)}) copy-start(f32[576,576]{0,1:T(8,128)} %copy-done.9) | copy-start | bytes 3981316
  406.6 124.0 %copy-start.3 = (f32[576,576]{1,0:T(8,128)S(1)}, f32[576,576]{1,0:T(8,128)}, u32[]{:S(2)}) copy-start(f32[576,576]{1,0:T(8,128)} %fusion.2) | copy-start | bytes 3981316
  530.6 6.1 %copy-start.24 = (f32[576,576]{1,0:T(8,128)S(1)}, f32[576,576]{1,0:T(8,128)}, u32[]{:S(2)}) copy-start(f32[576,576]{1,0:T(8,128)} %fusion.118) | copy-start | bytes 3981316
  530.6 6.1 %copy-start.30 = (f32[576,576]{1,0:T(8,128)S(1)}, f32[576,576]{1,0:T(8,128)}, u32[]{:S(2)}) copy-start(f32[576,576]{1,0:T(8,128)} %get-tuple-element.50) | copy-start | bytes 3981316
  536.7 5.4 copy-start.1
  536.7 5.3 copy-start.29
  542.1 4.5 copy-start.23
  542.1 4.5 copy-start.28
Sparse Core Ops, SparseCore 0:
  9.8 33.1 all-gather.15
  108.3 39.4 all-gather.7
  172.7 39.4 all-gather.9
  249.5 39.3 all-gather.11
  290.9 109.1 all-gather.13
  402.5 128.0 all-reduce.4
